TPU v7x, 32 devices: a whole 2x2x4 slice. The times are simulated.
32 devices in a mesh: grp: 2 (over x), tm: 16 (over z, y, core).
Axes of the slice: x: 2, y: 2, z: 4, core: 2. Of those that a mesh axis runs over, the one named last changes fastest.
Arguments:
- signals: bfloat16 [8, 1024, 256], P('grp', 'tm'), parts along dimension 0, may hold values from -6 to 6
- targets: bfloat16 [8, 1024, 768], P('grp', 'tm'), parts along dimension 0, may hold values from -6 to 6
- decay_rate: float32 [4096], P('grp'), parts along dimension 0, may hold values from 0 to 0.125, as said below
- pole_angle: float32 [4096], P('grp'), parts along dimension 0, may hold values from -3.1416 to 3.1416
- in_map: bfloat16 [8192, 256], P('grp'), parts along dimension 0
- out_map: bfloat16 [8192, 768], P('grp'), parts along dimension 0
Outputs:
- out_update: float32 [8192, 768], P(('grp', 'tm')), parts along dimension 0
- in_update: float32 [8192, 256], P(('grp', 'tm')), parts along dimension 0
- boundary_adjoint: float32 [8, 16, 4096], P('grp', 'tm'), parts along dimension 0
There are 2 independent parts, one for each index of `grp`. A program takes and returns all parts, laid end to end along the dimension named above; each array names one. Nothing has to cross between parts.
Inputs may be any that keep to these rules, and one draw needn't show every extreme that they name: Every mode decays: exp(-decay_rate) lies below 1.
All inputs are finite; a program needn't handle non-finite values.
Results may differ from a plain program's by a relative error of at most 0.0027.
Values sent between devices are 32-bit elements; how exact they have to be, the bound alone decides.
A program may use at most 128 MiB of HBM per device.

v0:
```python
import math

import jax
import jax.numpy as jnp
from jax import lax
from jax.sharding import PartitionSpec as P


def cmul(first, second):
    half = first.shape[-1] // 2
    fr = first[..., :half]
    fi = first[..., half:]
    sr = second[..., :half]
    si = second[..., half:]
    return jnp.concatenate([fr * sr - fi * si, fr * si + fi * sr], axis=-1)


def mode_powers(decay_rate, angle, unit, counts):
    phase = jnp.mod(angle * unit, 2.0 * math.pi) * counts
    magnitude = jnp.exp(-decay_rate * unit * counts)
    return jnp.concatenate([magnitude * jnp.cos(phase), magnitude * jnp.sin(phase)], axis=-1)


def per_device(signals, targets, decay_rate, pole_angle, in_map, out_map):
    group = signals.shape[1]
    modes = decay_rate.shape[0]
    width = 2 * modes
    position = lax.axis_index("tm")
    rate_row = decay_rate[None, :]
    fwd_angle = pole_angle[None, :]
    rev_angle = -pole_angle[None, :]
    gain = jnp.sqrt(-jnp.expm1(-2.0 * decay_rate))
    gain_pair = jnp.concatenate([gain, gain])
    unit_one = jnp.ones((1, 1), jnp.float32)
    drive = (
        lax.dot_general(
            signals, in_map, (((2,), (1,)), ((), ())), preferred_element_type=jnp.float32
        )
        * gain_pair
    )
    local = drive
    span = 1
    while span < group:
        factor = mode_powers(rate_row, fwd_angle, float(span), unit_one)
        local = jnp.concatenate(
            [local[:, :span], local[:, span:] + cmul(factor[None], local[:, :-span])], axis=1
        )
        span = span * 2
    ends = local[:, group - 1]
    piece = lax.all_gather(ends[None], "tm", axis=0, tiled=True)
    index = jnp.arange(piece.shape[0], dtype=jnp.int32)
    gap = position - 1 - index
    used = (gap >= 0).astype(jnp.float32)[:, None]
    counts = jnp.maximum(gap, 0).astype(jnp.float32)[:, None]
    weights = mode_powers(rate_row, fwd_angle, float(group), counts) * used
    entering = jnp.sum(cmul(weights[:, None, :], piece), axis=0)
    offsets = (jnp.arange(group, dtype=jnp.float32) + 1.0)[:, None]
    fwd_table = mode_powers(rate_row, fwd_angle, 1.0, offsets)
    states = local + cmul(fwd_table[None], entering[:, None, :])
    states_b = states.astype(jnp.bfloat16)
    predicted = lax.dot_general(
        states_b, out_map, (((2,), (0,)), ((), ())), preferred_element_type=jnp.float32
    )
    misfit_b = (predicted - targets.astype(jnp.float32)).astype(jnp.bfloat16)
    back = lax.dot_general(
        misfit_b, out_map, (((2,), (1,)), ((), ())), preferred_element_type=jnp.float32
    )
    retro = back
    span = 1
    while span < group:
        factor = mode_powers(rate_row, rev_angle, float(span), unit_one)
        retro = jnp.concatenate(
            [retro[:, :-span] + cmul(factor[None], retro[:, span:]), retro[:, group - span :]],
            axis=1,
        )
        span = span * 2
    starts = retro[:, 0]
    piece = lax.all_gather(starts[None], "tm", axis=0, tiled=True)
    index = jnp.arange(piece.shape[0], dtype=jnp.int32)
    gap = index - position - 1
    used = (gap >= 0).astype(jnp.float32)[:, None]
    counts = jnp.maximum(gap, 0).astype(jnp.float32)[:, None]
    weights = mode_powers(rate_row, rev_angle, float(group), counts) * used
    later = jnp.sum(cmul(weights[:, None, :], piece), axis=0)
    remaining = (float(group) - jnp.arange(group, dtype=jnp.float32))[:, None]
    rev_table = mode_powers(rate_row, rev_angle, 1.0, remaining)
    adjoint = retro + cmul(rev_table[None], later[:, None, :])
    scaled = adjoint * gain_pair
    adjoint_b = scaled.astype(jnp.bfloat16)
    boundary_adjoint = scaled[:, 0:1, :]
    joined = lax.psum_scatter(
        jnp.concatenate(
            [
                lax.dot_general(
                    states_b,
                    misfit_b,
                    (((0, 1), (0, 1)), ((), ())),
                    preferred_element_type=jnp.float32,
                ),
                lax.dot_general(
                    adjoint_b,
                    signals,
                    (((0, 1), (0, 1)), ((), ())),
                    preferred_element_type=jnp.float32,
                ),
            ],
            axis=1,
        ),
        "tm",
        scatter_dimension=0,
        tiled=True,
    )
    out_grad = joined[:, : out_map.shape[1]]
    in_grad = joined[:, out_map.shape[1] :]
    out_square, in_square = lax.psum(
        (jnp.sum(out_grad * out_grad), jnp.sum(in_grad * in_grad)), "tm"
    )
    out_update = out_grad * lax.rsqrt(out_square / float(width * out_map.shape[1]) + 1e-06)
    in_update = in_grad * lax.rsqrt(in_square / float(width * in_map.shape[1]) + 1e-06)
    return (out_update, in_update, boundary_adjoint)


def solution(mesh):
    return jax.shard_map(
        per_device,
        mesh=mesh,
        in_specs=(
            P("grp", "tm", None),
            P("grp", "tm", None),
            P("grp"),
            P("grp"),
            P("grp", None),
            P("grp", None),
        ),
        out_specs=(P(("grp", "tm"), None), P(("grp", "tm"), None), P("grp", "tm", None)),
        check_vma=False,
    )
```

profile of v0, /device:TPU:0, one launch (start us, length us, event | category | flops | bytes accessed | tf_op | source)
XLA Modules:
  0.0 378.4 jit_solution(7007309276360066433)
XLA Ops:
  7.2 1.3 cosine_multiply_fusion
  8.8 1.6 convolution_multiply_fusion
  10.5 0.9 multiply_subtract_fusion.7
  11.4 1.0 slice_add_fusion.5
  12.4 1.0 multiply_subtract_fusion.6
  13.4 1.0 slice_add_fusion.4
  14.4 0.7 fusion.4
  15.2 0.9 multiply_subtract_fusion.5
  16.0 1.0 slice_add_fusion.3
  17.1 0.7 multiply_subtract_fusion.9
  17.7 0.8 slice_add_fusion.7
  20.4 1.7 fusion.15
  22.1 0.7 slice.443
  23.1 0.6 fusion.44
  23.8 0.6 fusion.39
  25.0 0.6 fusion.41
  26.9 1.0 fusion.36
  27.9 0.8 maximum_multiply_fusion
  28.8 3.9 %fusion.29 = (f32[64,2048]{1,0:T(8,128)S(1)}, f32[64,2048]{1,0:T(8,128)S(1)}, f32[64,2048]{1,0:T(8,128)S(1)}, f32[64,2048]{1,0:T(8,128)S(1)}) fusion(f32[2048]{0:T(1024)S(1)} %get-tuple-element.116, f32[64]{0:T(128)S(1)} %iota_subtract_fusion, f32[2048]{0:T(1024)S(1)} %get-tuple-element.118, f32[2048]{0:T(1024)S(1)} %get-tuple-element.123, ...), kind=kLoop, calls=%fused_computation.110 | loop fusion | flops 1048576 | bytes 2122240 | tf_op jit(solution)/shard_map/mul | solution.py:21
  32.6 1.1 maximum_bitcast_fusion
  33.8 1.1 slice_bitcast_fusion.3
  34.8 28.8 %all-gather.5.cloned.1.call-done = f32[64,1,4096]{2,1,0:T(1,128)} async-done(((f32[4,1,4096]{2,1,0:T(1,128)}), f32[64,1,4096]{2,1,0:T(1,128)}) %all-gather.5.cloned.1.call-update) | async-done | bytes 1048592 | tf_op jit(solution)/shard_map/all_gather | solution.py:50
  63.6 3.7 reduce
  67.4 1.3 reshape.510
  68.7 1.6 multiply_subtract_fusion.15
  70.5 0.6 multiply_subtract_fusion.4
  71.2 0.9 copy-done.9
  72.1 0.9 fusion.11
  73.0 1.3 copy-done.5
  74.4 1.8 fusion.23
  76.2 2.1 fusion
  78.4 0.9 multiply_subtract_fusion.3
  79.2 0.7 slice_add_fusion.2
  79.9 1.1 multiply_subtract_fusion.2
  81.0 0.7 slice_add_fusion.1
  82.4 0.7 multiply_subtract_fusion.1
  83.1 0.7 slice_add_fusion
  83.8 0.6 multiply_subtract_fusion.8
  88.1 1.3 copy-done.7
  89.4 0.7 slice.487
  90.4 1.9 slice_bitcast_fusion.5
  92.2 2.3 slice_bitcast_fusion.1
  94.5 6.4 %convolution_bitcast_fusion = f32[4096,768]{0,1:T(8,128)} fusion(bf16[4,64,4096]{2,1,0:T(8,128)(2,1)S(1)} %copy-done.6, bf16[4,64,768]{2,1,0:T(8,128)(2,1)S(1)} %fusion.23), kind=kOutput, calls=%fused_computation.7 | convolution fusion | flops 1610612736 | bytes 15073280 | tf_op jit(solution)/shard_map/dot_general | solution.py:94
  100.9 26.2 %all-gather.7.cloned.1.call-done = f32[64,1,4096]{2,1,0:T(1,128)} async-done(((f32[4,1,4096]{2,1,0:T(1,128)}), f32[64,1,4096]{2,1,0:T(1,128)}) %all-gather.7.cloned.1.call-update) | async-done | bytes 1048592 | tf_op jit(solution)/shard_map/all_gather | solution.py:78
  127.1 4.8 %reduce.1 = f32[64,4096]{1,0:T(8,128)} reduce(f32[64,1,4096]{2,1,0:T(1,128)} %all-gather.7.cloned.1.call-done, f32[]{:T(128)} %constant.75), dimensions={1}, to_apply=%all-gather.1.reduce_sub_computation | reduce | bytes 2097156 | tf_op jit(solution)/shard_map/all_gather | solution.py:78
  131.8 2.5 reshape.511
  134.4 1.6 multiply_subtract_fusion.14
  136.2 0.6 multiply_subtract_fusion
  137.4 0.7 copy-done.8
  138.1 0.6 fusion.9
  138.8 2.1 copy-done.2
  140.9 0.8 convolution_bitcast_fusion.1
  141.9 1.3 slice-done.1
  143.2 1.4 slice-done.2
  144.6 6.1 %pad_maximum_fusion = f32[4096,1024]{0,1:T(8,128)} fusion(f32[4096,256]{0,1:T(8,128)S(1)} %convolution_bitcast_fusion.1, f32[4096,768]{0,1:T(8,128)S(1)} %bitcast.133), kind=kLoop, calls=%fused_computation | loop fusion | flops 4194304 | bytes 33554432 | tf_op jit(solution)/shard_map/concatenate | solution.py:92
  150.7 177.6 %reduce-scatter.2.cloned.1.call-done = f32[256,1024]{0,1:T(8,128)} async-done(((f32[4096,1024]{0,1:T(8,128)}), f32[256,1024]{0,1:T(8,128)}) %reduce-scatter.2.cloned.1.call-update) | async-done | bytes 1048592 | tf_op jit(solution)/shard_map/reduce_scatter | solution.py:91
  328.3 1.6 multiply_reduce_fusion.1
  329.9 1.9 multiply_reduce_fusion
  331.9 1.7 slice.496
  333.6 32.1 %all-reduce = (f32[]{:T(128)}, f32[]{:T(128)}) all-reduce(f32[]{:T(128)} %multiply_reduce_fusion, f32[]{:T(128)} %multiply_reduce_fusion.1), channel_id=1, replica_groups=mesh['grp'=2,'tm'=16] {'tm'}, use_global_device_ids=true, to_apply=%region_4.5 | all-reduce | flops 2 | bytes 16 | tf_op jit(solution)/shard_map/psum | solution.py:115
  367.1 1.3 slice_multiply_fusion
  368.4 1.1 copy.11
  369.6 1.0 slice_multiply_fusion.1
  370.6 0.8 copy.12
  (123 shorter events, 10.3 us)
Async XLA Ops:
  7.2 1.6 copy-start
  7.2 56.5 %all-gather.5.cloned.1.call-start = ((), (), s32[]{:S(2)}) async-start(), calls=%async_computation.2 | async-start | bytes 1114112 | tf_op jit(solution)/shard_map/all_gather | solution.py:50
  22.8 104.3 %all-gather.7.cloned.1.call-start = ((), (), s32[]{:S(2)}) async-start(), calls=%async_computation.3 | async-start | bytes 1114112 | tf_op jit(solution)/shard_map/all_gather | solution.py:78
  68.7 1.8 copy-start.12
  68.7 1.8 copy-start.13
  70.5 1.6 copy-start.9
  70.5 3.8 %slice-start.3 = ((s8[6291456]{0:T(1024)(128)(4,1)}), s8[4194304]{0:T(1024)(128)(4,1)S(1)}, s32[]{:S(2)}) async-start(s8[6291456]{0:T(1024)(128)(4,1)} %bitcast.134), calls=%async_computation.7 | async-start | bytes 8388608
  72.1 2.2 slice-start.4
  72.1 2.3 copy-start.29
  73.0 1.3 copy-start.5
  76.2 2.2 copy-start.23
  76.2 2.2 copy-start.24
  79.2 0.7 copy-start.27
  79.2 0.7 copy-start.28
  81.7 0.7 copy-start.25
  81.7 0.7 copy-start.26
  83.1 0.7 copy-start.21
  83.1 0.7 copy-start.22
  85.3 0.7 copy-start.19
  85.3 0.7 copy-start.20
  85.4 1.5 copy-start.3
  86.5 0.7 copy-start.17
  86.5 0.7 copy-start.18
  88.1 1.3 copy-start.7
  90.1 238.2 %reduce-scatter.2.cloned.1.call-start = ((), (), s32[]{:S(2)}) async-start(), calls=%async_computation.1 | async-start | bytes 17825792 | tf_op jit(solution)/shard_map/reduce_scatter | solution.py:91
  90.4 4.1 %copy-start.6 = (bf16[4,64,4096]{2,1,0:T(8,128)(2,1)S(1)}, bf16[4,64,4096]{2,1,0:T(8,128)(2,1)}, u32[]{:S(2)}) copy-start(bf16[4,64,4096]{2,1,0:T(8,128)(2,1)} %copy-done.5) | copy-start | bytes 6291460
  100.9 33.4 %copy-start.15 = (f32[16,2048]{1,0:T(8,128)S(1)}, f32[16,2048]{1,0:T(8,128)}, u32[]{:S(2)}) copy-start(f32[16,2048]{1,0:T(8,128)} %get-tuple-element.50) | copy-start | bytes 393220
  100.9 33.4 %copy-start.16 = (f32[16,2048]{1,0:T(8,128)S(1)}, f32[16,2048]{1,0:T(8,128)}, u32[]{:S(2)}) copy-start(f32[16,2048]{1,0:T(8,128)} %get-tuple-element.51) | copy-start | bytes 393220
  134.4 1.8 copy-start.10
  134.4 1.8 copy-start.11
  136.2 1.2 copy-start.4
  136.2 1.9 copy-start.8
  138.1 2.8 copy-start.14
  138.1 3.8 slice-start
  138.1 5.0 %slice-start.1 = ((s8[12582912]{0:T(1024)(128)(4,1)}), s8[4194304]{0:T(1024)(128)(4,1)S(1)}, s32[]{:S(2)}) async-start(s8[12582912]{0:T(1024)(128)(4,1)} %bitcast.132), calls=%async_computation.5 | async-start | bytes 8388608
  138.8 2.1 copy-start.2
  140.9 3.7 slice-start.2
  367.1 4.3 %copy-start.1 = (bf16[4096,256]{1,0:T(8,128)(2,1)S(1)}, bf16[4096,256]{1,0:T(8,128)(2,1)}, u32[]{:S(2)}) copy-start(bf16[4096,256]{1,0:T(8,128)(2,1)} %param.10) | copy-start | bytes 6291460
Sparse Core Ops, SparseCore 0:
  22.9 40.6 all-gather.4
  90.2 36.8 all-gather.6
  150.8 177.4 reduce-scatter.1
where the time goes:
time: 386 us; the launch traced here: 378 us
  waiting for transfers between devices  233 us (60%)
  other arithmetic  54.7 us (14%)
  blocking collectives  32.1 us (8%)
  local copies, waits for them, and re-layouts  29.3 us (8%)
  between operations  16.4 us (4%)
  matrix products  12.7 us (3%)
    reduce_scatter x1, waiting for transfers between devices, per_device(): lax.psum_scatter(jnp.concatenate([lax.dot_general(states_b, misfit_b, (((...  178 us
    psum x1, blocking collectives, per_device(): lax.psum((jnp.sum(out_grad * out_grad), jnp.sum(in_grad * in_grad)), 'tm')  32.1 us
    all_gather x1, waiting for transfers between devices, per_device(): piece = lax.all_gather(ends[None], 'tm', axis=0, tiled=True)  28.8 us
    all_gather x1, waiting for transfers between devices, per_device(): piece = lax.all_gather(starts[None], 'tm', axis=0, tiled=True)  26.2 us
    unnamed x72, local copies, waits for them, and re-layouts  13.2 us
    sub x16, other arithmetic, cmul(): return jnp.concatenate([fr * sr - fi * si, fr * si + fi * sr], axis=-1)  12.4 us
  transfers between devices with their start and end apart: 3, of which 3 were waited for; matrix products, arithmetic and copies ran while one was open for 6% of the time, Pallas kernels for 0%

commit v1 on v0

v1 whole, which is shorter than its diff:
```python
import functools

import jax
import jax.numpy as jnp
from jax import lax
from jax.experimental import pallas as pl
from jax.experimental.pallas import tpu as pltpu
from jax.sharding import PartitionSpec as P

F32 = jnp.float32
BF16 = jnp.bfloat16
MESH = pl.DeviceIdType.MESH
COLS = 256


def remote(src, dst, send_sem, recv_sem, device):
    return pltpu.make_async_remote_copy(
        src_ref=src,
        dst_ref=dst,
        send_sem=send_sem,
        recv_sem=recv_sem,
        device_id={"tm": device},
        device_id_type=MESH,
    )


def cmul(ar, ai, br, bi):
    return ar * br - ai * bi, ar * bi + ai * br


class Chain:
    def __init__(self, n, pos, device_of, chunk, slots, send, recv):
        self.n, self.pos, self.device_of, self.chunk = n, pos, device_of, chunk
        self.slots, self.send, self.recv = slots, send, recv

    def turn(self, s, first):
        n, p = self.n, self.pos
        low = 2 * p < n
        right = low if first else jnp.logical_not(low)
        c = jnp.where(right, n - 1 - s, s)
        go = jnp.where(right, c > p, c < p)
        has = jnp.where(right, p > 0, p < n - 1)
        to = jnp.where(right, p + 1, p - 1)
        slot = jnp.where(right, c, jnp.where(c == p - 1, n, c))
        return c, go, has, to, slot

    def copy(self, c, slot, to):
        return remote(
            self.chunk(c), self.slots.at[slot], self.send.at[c], self.recv.at[slot], self.device_of(to)
        )

    def arrive(self, slot):
        self.copy(slot % self.n, slot, self.pos).wait_recv()

    def step(self, s):
        for first in (True, False):
            c, go, has, to, slot = self.turn(s, first)

            @pl.when(jnp.logical_and(go, has))
            def _():
                self.arrive(c)
                mine = self.chunk(c)
                mine[...] = mine[...] + self.slots[c]

            @pl.when(go)
            def _():
                self.copy(c, slot, to).start()

    def finish(self):
        n, p = self.n, self.pos
        mine = self.chunk(p)

        @pl.when(p > 0)
        def _():
            self.arrive(p)
            mine[...] = mine[...] + self.slots[p]

        @pl.when(p < n - 1)
        def _():
            self.arrive(n)
            mine[...] = mine[...] + self.slots[n]

    def drain(self):
        for c in range(self.n):

            @pl.when(self.pos != c)
            def _():
                self.copy(c, c, self.pos).wait_send()


def kernel(
    na, nb, group, rows,
    sig_ref, tgt_ref, pole_ref, gain_ref, in_hbm, out_hbm,
    upd_ref, upi_ref, bnd_ref, bnr_ref,
    inm, outm, sig_in, sig_b, work, st_b, ad_b, d_out, d_in, mis,
    e_out, e_in, f_out, f_in, sq_out, sq_in,
    gp, ys, zs, zz, zy,
    ld_sem, pair_send, pair_recv, es, er, fs, fr, qs, qr,
    ysend, yrecv, zsend, zrecv, zzsend, zzrecv, zysend, zyrecv,
):
    chips = na * nb
    n_tm = 2 * chips
    me = lax.axis_index("tm")
    core = me % 2
    chip = me // 2
    pa = chip // nb
    pb = chip % nb
    mate = chip * 2 + 1 - core
    half = pole_ref.shape[2]
    width = 2 * half
    lines = 8 * group
    n_out = outm.shape[1] // COLS

    loads = []
    for q in range(chips):
        loads.append(
            pltpu.make_async_copy(in_hbm.at[q, core], inm.at[pl.ds(q * rows, rows)], ld_sem.at[0, q])
        )
        loads.append(
            pltpu.make_async_copy(out_hbm.at[q, core], outm.at[pl.ds(q * rows, rows)], ld_sem.at[1, q])
        )
    for load in loads:
        load.start()

    barrier = pltpu.get_barrier_semaphore()

    def greet(k, _):
        other = (me + k) % n_tm
        pl.semaphore_signal(barrier, inc=1, device_id={"tm": other}, device_id_type=MESH)
        return 0

    lax.fori_loop(1, n_tm, greet, 0)
    pl.semaphore_wait(barrier, n_tm - 1)

    sig_copy = remote(sig_ref, sig_in, pair_send.at[0], pair_recv.at[0], mate)
    sig_copy.start()
    for load in loads:
        load.wait()
    sig_copy.wait()
    sig_b[...] = (sig_ref[...] + sig_in[...]).astype(BF16)

    def drive_block(i, _):
        at = pl.ds(pl.multiple_of(i * COLS, COLS), COLS)
        val = lax.dot_general(
            sig_b[...], inm[at, :], (((1,), (1,)), ((), ())), preferred_element_type=F32
        )
        work[:, :, at] = val.reshape(group, 8, COLS) * gain_ref[:, at][None]
        return 0

    lax.fori_loop(0, width // COLS, drive_block, 0)

    pr = pole_ref[0]
    pi = pole_ref[1]
    gr, gi = pr, pi
    span = 1
    while span < group:
        gr, gi = cmul(gr, gi, gr, gi)
        span *= 2
    hr, hi = cmul(gr, gi, gr, gi)
    g4r, g4i, h4r, h4i = gr[:4], gi[:4], hr[:4], hi[:4]
    zero = jnp.zeros((8, half), F32)

    def ends_step(t, carry):
        r, m = carry
        a, b = cmul(pole_ref[0], pole_ref[1], r, m)
        return a + work[t, :, :half], b + work[t, :, half:]

    er_, ei_ = lax.fori_loop(0, group, ends_step, (zero, zero), unroll=2)
    cr, ci = cmul(g4r, g4i, er_[:4], ei_[:4])
    e_out[:4, :] = cr + er_[4:]
    e_out[4:, :] = ci + ei_[4:]

    def send_fwd(q, _):
        remote(e_out, e_in.at[chip], es.at[q], er.at[chip], q * 2 + core).start()
        return 0

    lax.fori_loop(chip + 1, chips, send_fwd, 0)

    def take_fwd(q, carry):
        r, m = carry
        remote(e_out, e_in.at[q], es.at[q], er.at[q], mate).wait_recv()
        a, b = cmul(h4r, h4i, r, m)
        return a + e_in[q, :4, :], b + e_in[q, 4:, :]

    z4 = jnp.zeros((4, half), F32)
    xr, xi = lax.fori_loop(0, chip, take_fwd, (z4, z4))
    ur, ui = cmul(g4r, g4i, xr, xi)
    sr0 = jnp.concatenate([xr, ur + er_[:4]], axis=0)
    si0 = jnp.concatenate([xi, ui + ei_[:4]], axis=0)

    def state_step(k, carry):
        r, m = carry
        rs, ms = [], []
        for j in range(2):
            a, b = cmul(pole_ref[0], pole_ref[1], r, m)
            r = a + work[2 * k + j, :, :half]
            m = b + work[2 * k + j, :, half:]
            rs.append(r)
            ms.append(m)
        at = pl.ds(pl.multiple_of(k * 16, 16), 16)
        st_b[at, :half] = jnp.concatenate(rs, axis=0).astype(BF16)
        st_b[at, half:] = jnp.concatenate(ms, axis=0).astype(BF16)
        return r, m

    lax.fori_loop(0, group // 2, state_step, (sr0, si0))

    swaps = []
    for k in range(n_out):
        at = pl.ds(k * COLS, COLS)
        val = jnp.dot(st_b[...], outm[:, at], preferred_element_type=F32)
        d_out[k] = val - tgt_ref[:, at]
        swap = remote(d_out.at[k], d_in.at[k], pair_send.at[1 + k], pair_recv.at[1 + k], mate)
        swap.start()
        swaps.append(swap)

    def grad(k, left, right):
        for i in range(width // COLS):
            val = lax.dot_general(
                left[:, pl.ds(i * COLS, COLS)], right, (((0,), (0,)), ((), ())),
                preferred_element_type=F32,
            )
            if rows >= COLS:
                per = rows // COLS
                q = i // per
                gp[k, q // nb, q % nb, pl.ds((i % per) * COLS, COLS), :] = val
            else:
                for j in range(COLS // rows):
                    q = i * (COLS // rows) + j
                    gp[k, q // nb, q % nb] = val[j * rows : (j + 1) * rows]

    def a_dev(a):
        return (a * nb + pb) * 2 + core

    def b_dev(b):
        return (pa * nb + b) * 2 + core

    first_a = Chain(na, pa, a_dev, lambda c: gp.at[0, c], zz, zzsend, zzrecv)
    then_b = Chain(nb, pb, b_dev, lambda c: gp.at[0, pa, c], zy, zysend, zyrecv)
    bs = [
        Chain(nb, pb, b_dev, lambda c, k=k: gp.at[k, :, c], ys.at[k - 1], ysend.at[k - 1], yrecv.at[k - 1])
        for k in range(1, n_out + 1)
    ]
    as_ = [
        Chain(na, pa, a_dev, lambda c, k=k: gp.at[k, c, pb], zs.at[k - 1], zsend.at[k - 1], zrecv.at[k - 1])
        for k in range(1, n_out + 1)
    ]

    def run(chain, lo, hi):
        def body(s, _):
            chain.step(s)
            return 0

        lax.fori_loop(lo, hi, body, 0)

    for k in range(n_out):
        swaps[k].wait()
        mis[:, k * COLS : (k + 1) * COLS] = (d_out[k] + d_in[k]).astype(BF16)
        grad(k, st_b, mis[:, k * COLS : (k + 1) * COLS])
        if k == 0:
            first_a.step(0)
        elif k == 1:
            run(bs[0], 0, nb - 1)

    def back_block(i, _):
        at = pl.ds(pl.multiple_of(i * COLS, COLS), COLS)
        val = lax.dot_general(
            mis[...], outm[at, :], (((1,), (1,)), ((), ())), preferred_element_type=F32
        )
        work[:, :, at] = val.reshape(group, 8, COLS)
        return 0

    lax.fori_loop(0, width // COLS, back_block, 0)

    def cmulc(ar, ai, br, bi):
        return ar * br + ai * bi, ar * bi - ai * br

    def starts_step(k, carry):
        t = group - 1 - k
        r, m = carry
        a, b = cmulc(pole_ref[0], pole_ref[1], r, m)
        return a + work[t, :, :half], b + work[t, :, half:]

    br_, bi_ = lax.fori_loop(0, group, starts_step, (zero, zero), unroll=2)
    cr, ci = cmulc(g4r, g4i, br_[4:], bi_[4:])
    f_out[:4, :] = cr + br_[:4]
    f_out[4:, :] = ci + bi_[:4]

    def send_rev(q, _):
        remote(f_out, f_in.at[chip], fs.at[q], fr.at[chip], q * 2 + core).start()
        return 0

    lax.fori_loop(0, chip, send_rev, 0)

    def take_rev(k, carry):
        q = chips - 1 - k
        r, m = carry
        remote(f_out, f_in.at[q], fs.at[q], fr.at[q], mate).wait_recv()
        a, b = cmulc(h4r, h4i, r, m)
        return a + f_in[q, :4, :], b + f_in[q, 4:, :]

    xr, xi = lax.fori_loop(0, chips - 1 - chip, take_rev, (z4, z4))
    ur, ui = cmulc(g4r, g4i, xr, xi)
    ar0 = jnp.concatenate([ur + br_[4:], xr], axis=0)
    ai0 = jnp.concatenate([ui + bi_[4:], xi], axis=0)

    def adj_step(k, carry):
        r, m = carry
        k2 = group // 2 - 1 - k
        rs, ms = [], []
        for j in (1, 0):
            a, b = cmulc(pole_ref[0], pole_ref[1], r, m)
            r = a + work[2 * k2 + j, :, :half]
            m = b + work[2 * k2 + j, :, half:]
            rs.insert(0, r * gain_ref[:, :half])
            ms.insert(0, m * gain_ref[:, half:])
        at = pl.ds(pl.multiple_of(k2 * 16, 16), 16)
        ad_b[at, :half] = jnp.concatenate(rs, axis=0).astype(BF16)
        ad_b[at, half:] = jnp.concatenate(ms, axis=0).astype(BF16)
        return r, m

    ar_, ai_ = lax.fori_loop(0, group // 2, adj_step, (ar0, ai0))
    bnd_ref[:, :half] = ar_ * gain_ref[:, :half]
    bnd_ref[:, half:] = ai_ * gain_ref[:, half:]
    bnd_copy = remote(
        bnd_ref, bnr_ref, pair_send.at[1 + n_out], pair_recv.at[1 + n_out], mate
    )
    bnd_copy.start()

    grad(n_out, ad_b, sig_b[...])

    run(first_a, 1, na - 1)
    for k in range(n_out):
        bs[k].finish()
        if k + 1 < n_out:
            run(bs[k + 1], 0, nb - 1)
        if k == 0:
            first_a.finish()
            run(then_b, 0, nb - 1)
            run(as_[0], 0, na - 1)
        else:
            run(as_[k], 0, na - 1)
            as_[k - 1].finish()
    then_b.finish()
    as_[n_out - 1].finish()

    def part(x):
        v = jnp.sum((x * x).reshape(rows // 8, 8, COLS), axis=0)
        return v[:, :128] + v[:, 128:]

    total = part(gp[0, pa, pb])
    for k in range(1, n_out):
        total = total + part(gp[k, pa, pb])
    sq_out[0] = total
    sq_out[1] = part(gp[n_out, pa, pb])

    def send_sq(k, _):
        other = (me + k) % n_tm
        remote(sq_out, sq_in.at[me], qs.at[other], qr.at[me], other).start()
        return 0

    lax.fori_loop(1, n_tm, send_sq, 0)
    sq_in[me] = sq_out[...]

    def take_sq(k, _):
        other = (me + k) % n_tm
        remote(sq_out, sq_in.at[other], qs.at[other], qr.at[other], other).wait_recv()
        return 0

    lax.fori_loop(1, n_tm, take_sq, 0)
    sums = jnp.sum(sq_in[...], axis=0)
    count = 2.0 * width
    out_scale = lax.rsqrt(jnp.sum(sums[0], keepdims=True) / (count * COLS * n_out) + 1e-6)
    in_scale = lax.rsqrt(jnp.sum(sums[1], keepdims=True) / (count * COLS) + 1e-6)
    for k in range(n_out):
        upd_ref[:, k * COLS : (k + 1) * COLS] = gp[k, pa, pb] * out_scale
    upi_ref[...] = gp[n_out, pa, pb] * in_scale

    def sent_sq(k, _):
        other = (me + k) % n_tm
        remote(sq_out, sq_in.at[me], qs.at[other], qr.at[me], other).wait_send()
        return 0

    lax.fori_loop(1, n_tm, sent_sq, 0)

    def sent_fwd(q, _):
        remote(e_out, e_in.at[chip], es.at[q], er.at[chip], q * 2 + core).wait_send()
        return 0

    lax.fori_loop(chip + 1, chips, sent_fwd, 0)

    def sent_rev(q, _):
        remote(f_out, f_in.at[chip], fs.at[q], fr.at[chip], q * 2 + core).wait_send()
        return 0

    lax.fori_loop(0, chip, sent_rev, 0)
    bnd_copy.wait()
    for chain in [first_a, then_b] + bs + as_:
        chain.drain()


def per_device(na, nb, signals, targets, decay_rate, pole_angle, in_map, out_map):
    members, group, sensors = signals.shape
    modes = decay_rate.shape[0]
    chips = na * nb
    rows = in_map.shape[0] // (2 * chips)
    core = lax.axis_index("tm") % 2
    half = modes // 2
    width = modes
    n_out = out_map.shape[1] // COLS
    lines = 2 * members * group

    def padded(x):
        x = jnp.transpose(x, (1, 0, 2)).astype(F32)
        low = jnp.where(core == 0, x, 0.0)
        high = jnp.where(core == 0, 0.0, x)
        return jnp.concatenate([low, high], axis=1).reshape(lines, x.shape[2])

    def own(x):
        return lax.dynamic_index_in_dim(x.reshape(-1, 2, rows), core, 1, False).reshape(half)

    rate, angle = own(decay_rate), own(pole_angle)
    size = jnp.exp(-rate)
    pole = jnp.stack([size * jnp.cos(angle), size * jnp.sin(angle)])
    pole = jnp.broadcast_to(pole[:, None, :], (2, 8, half))
    gain = jnp.sqrt(-jnp.expm1(-2.0 * rate))
    gain = jnp.broadcast_to(jnp.concatenate([gain, gain])[None], (8, width))

    vm = pl.BlockSpec(memory_space=pltpu.VMEM)
    anyw = pl.BlockSpec(memory_space=pl.ANY)
    dma = pltpu.SemaphoreType.DMA
    scratch = [
        pltpu.VMEM((width, sensors), BF16),
        pltpu.VMEM((width, n_out * COLS), BF16),
        pltpu.VMEM((lines, sensors), F32),
        pltpu.VMEM((lines, sensors), BF16),
        pltpu.VMEM((group, 8, width), F32),
        pltpu.VMEM((lines, width), BF16),
        pltpu.VMEM((lines, width), BF16),
        pltpu.VMEM((n_out, lines, COLS), F32),
        pltpu.VMEM((n_out, lines, COLS), F32),
        pltpu.VMEM((lines, n_out * COLS), BF16),
        pltpu.VMEM((8, half), F32),
        pltpu.VMEM((chips, 8, half), F32),
        pltpu.VMEM((8, half), F32),
        pltpu.VMEM((chips, 8, half), F32),
        pltpu.VMEM((2, 8, 128), F32),
        pltpu.VMEM((2 * chips, 2, 8, 128), F32),
        pltpu.VMEM((n_out + 1, na, nb, rows, COLS), F32),
        pltpu.VMEM((n_out, nb + 1, na, rows, COLS), F32),
        pltpu.VMEM((n_out, na + 1, rows, COLS), F32),
        pltpu.VMEM((na + 1, nb, rows, COLS), F32),
        pltpu.VMEM((nb + 1, rows, COLS), F32),
        dma((2, chips)),
        dma((n_out + 2,)),
        dma((n_out + 2,)),
        dma((chips,)),
        dma((chips,)),
        dma((chips,)),
        dma((chips,)),
        dma((2 * chips,)),
        dma((2 * chips,)),
        dma((n_out, nb)),
        dma((n_out, nb + 1)),
        dma((n_out, na)),
        dma((n_out, na + 1)),
        dma((na,)),
        dma((na + 1,)),
        dma((nb,)),
        dma((nb + 1,)),
    ]
    upd, upi, bnd, bnr = pl.pallas_call(
        functools.partial(kernel, na, nb, group, rows),
        out_shape=(
            jax.ShapeDtypeStruct((rows, n_out * COLS), F32),
            jax.ShapeDtypeStruct((rows, sensors), F32),
            jax.ShapeDtypeStruct((8, width), F32),
            jax.ShapeDtypeStruct((8, width), F32),
        ),
        in_specs=[vm, vm, vm, vm, anyw, anyw],
        out_specs=(vm, vm, vm, vm),
        scratch_shapes=scratch,
        compiler_params=pltpu.CompilerParams(
            collective_id=0, has_side_effects=True, vmem_limit_bytes=62 * 1024 * 1024
        ),
    )(
        padded(signals),
        padded(targets),
        pole,
        gain,
        in_map.reshape(chips, 2, rows, sensors),
        out_map.reshape(chips, 2, rows, n_out * COLS),
    )
    bnd = lax.dynamic_slice_in_dim(bnd, core * members, members, 0).reshape(members, chips, rows)
    bnr = lax.dynamic_slice_in_dim(bnr, core * members, members, 0).reshape(members, chips, rows)
    even = jnp.where(core == 0, bnd, bnr)
    odd = jnp.where(core == 0, bnr, bnd)
    boundary = jnp.stack([even, odd], axis=2).reshape(members, 1, 2 * width)
    return upd, upi, boundary


def solution(mesh):
    chips = mesh.shape["tm"] // 2
    nb = 1
    while 4 * nb * nb <= chips:
        nb *= 2
    na = chips // nb
    return jax.shard_map(
        functools.partial(per_device, na, nb),
        mesh=mesh,
        in_specs=(
            P("grp", "tm", None),
            P("grp", "tm", None),
            P("grp"),
            P("grp"),
            P("grp", None),
            P("grp", None),
        ),
        out_specs=(P(("grp", "tm"), None), P(("grp", "tm"), None), P("grp", "tm", None)),
        check_vma=False,
    )
```

time: 386 us -> 167 us (0.43); the launches traced: 378 us -> 167 us
  waiting for transfers between devices: 233 us -> 0 us
  Pallas kernels: 0 us -> 155 us
  other arithmetic: 54.7 us -> 2.42 us
  blocking collectives: 32.1 us -> 0 us
  local copies, waits for them, and re-layouts: 29.3 us -> 8.03 us
  between operations: 16.4 us -> 0.76 us
  matrix products: 12.7 us -> 0 us
    reduce_scatter x1 -> x0, waiting for transfers between devices: 178 us -> none  [per_device(): lax.psum_scatter(jnp.concatenate([lax.dot_general(states_b, misfit_b, (((...]
    pallas_call x0 -> x1, Pallas kernels: none -> 155 us  [per_device(): pl.pallas_call(functools.partial(kernel, na, nb, group, rows), out_shape=...]
    all_gather x2 -> x0, waiting for transfers between devices: 55 us -> none  [the longest x1 28.8 us: per_device(): piece = lax.all_gather(ends[None], 'tm', axis=0, tiled=True)]
    psum x1 -> x0, blocking collectives: 32.1 us -> none  [per_device(): lax.psum((jnp.sum(out_grad * out_grad), jnp.sum(in_grad * in_grad)), 'tm')]
    dot_general x5 -> x0, matrix products: 12.7 us -> none  [the longest x1 6.4 us: per_device(): lax.dot_general(states_b, misfit_b, (((0, 1), (0, 1)), ((), ())), preferr...]
    sub x17 -> x0, other arithmetic: 12.5 us -> none  [the longest x16 12.4 us: cmul(): return jnp.concatenate([fr * sr - fi * si, fr * si + fi * sr], axis=-1)]
    concatenate x8 -> x3, other arithmetic: 10.7 us -> 0.15 us  [the longest x2 0.15 us: padded(): return jnp.concatenate([low, high], axis=1).reshape(lines, x.shape[2])]
    unnamed x72 -> x10, local copies, waits for them, and re-layouts: 13.2 us -> 2.78 us
  transfers between devices with their start and end apart: 3 -> 0, of which waited for: 3 -> 0; matrix products, arithmetic and copies ran while one was open for 6% -> 0% of each run, Pallas kernels for 0% -> 0%
where the time goes in v1:
time: 167 us
  Pallas kernels  155 us (93%)
  local copies, waits for them, and re-layouts  8.03 us (5%)
  other arithmetic  2.42 us (1%)
    pallas_call x1, Pallas kernels, per_device(): pl.pallas_call(functools.partial(kernel, na, nb, group, rows), out_shape=...  155 us

profile of v1, /device:TPU:0, one launch (start us, length us, event | category | flops | bytes accessed | tf_op | source)
XLA Modules:
  0.0 166.5 jit_solution(5723510693621062756)
XLA Ops:
  0.6 1.1 fusion
  1.8 0.1 pad_maximum_fusion
  1.9 0.0 copy-start.1
  1.9 2.1 %copy.21 = f32[64,8,768]{2,1,0:T(8,128)} copy(f32[64,8,768]{2,0,1:T(8,128)S(1)} %pad_maximum_fusion) | data formatting | bytes 3145728 | tf_op jit(solution)/shard_map/concatenate | solution.py:416
  4.0 0.0 copy-start.2
  4.0 0.0 copy-start.3
  4.0 0.0 copy-done.1
  4.1 1.1 copy.22
  5.2 0.0 copy-done.2
  5.2 0.0 copy-done.3
  5.2 0.2 cosine_multiply_fusion
  5.4 0.6 broadcast_in_dim.26.pole_ref
  6.0 0.6 broadcast_in_dim.27.gain_ref
  6.7 155.3 %shard_map.85 = (f32[256,768]{1,0:T(8,128)}, f32[256,256]{1,0:T(8,128)}, f32[8,2048]{1,0:T(8,128)}, f32[8,2048]{1,0:T(8,128)}) custom-call(f32[512,256]{1,0:T(8,128)} %bitcast.32, f32[512,768]{1,0:T(8,128)} %bitcast.30, f32[2,8,1024]{2,1,0:T(8,128)} %broadcast_in_dim.26.pole_ref, f32[8,2048]{1,0:T(8,128)} %broadcast_in_dim.27.gain_ref, ...), custom_call_target="tpu_custom_call" | custom-call | tf_op jit(solution)/shard_map/pallas_call | solution.py:471
  162.0 0.0 copy-start
  162.0 0.9 dynamic-slice_select_fusion.1
  163.0 0.1 copy.14
  163.0 0.7 reshape.133
  163.8 2.1 %copy.25 = f32[256,768]{1,0:T(8,128)} copy(f32[256,768]{1,0:T(8,128)} %get-tuple-element.25) | data formatting | bytes 1572864
  165.8 0.0 copy-done
  165.8 0.7 copy.26
  (8 shorter events, 0.1 us)
Async XLA Ops:
  1.9 2.1 %copy-start.1 = (bf16[4,64,256]{2,1,0:T(8,128)(2,1)S(1)}, bf16[4,64,256]{2,1,0:T(8,128)(2,1)}, u32[]{:S(2)}) copy-start(bf16[4,64,256]{2,1,0:T(8,128)(2,1)} %param.6) | copy-start | bytes 393220
  4.0 1.2 copy-start.2
  4.0 1.2 copy-start.3
  162.0 3.8 %copy-start = (f32[256,256]{1,0:T(8,128)S(1)}, f32[256,256]{1,0:T(8,128)}, u32[]{:S(2)}) copy-start(f32[256,256]{1,0:T(8,128)} %get-tuple-element.26) | copy-start | bytes 786436

commit v2 on v1

--- a/solution.py
+++ b/solution.py
@@ -33,38 +33,49 @@
         self.n, self.pos, self.device_of, self.chunk = n, pos, device_of, chunk
         self.slots, self.send, self.recv = slots, send, recv
 
-    def turn(self, s, first):
+    def copy(self, c, slot, to):
+        return remote(
+            self.chunk(c), self.slots.at[slot], self.send.at[c], self.recv.at[slot], self.device_of(to)
+        )
+
+    def arrive(self, slot):
+        self.copy(slot % self.n, slot, self.pos).wait_recv()
+
+    def launch(self, c, right):
+        to = jnp.where(right, self.pos + 1, self.pos - 1)
+        slot = jnp.where(jnp.logical_and(jnp.logical_not(right), c == self.pos - 1), self.n, c)
+        self.copy(c, slot, to).start()
+
+    def lead(self):
+        n, p = self.n, self.pos
+
+        @pl.when(jnp.logical_or(p == 0, p == n - 1))
+        def _():
+            def body(s, _):
+                right = p == 0
+                self.launch(jnp.where(right, n - 1 - s, s), right)
+                return 0
+
+            lax.fori_loop(0, n - 1, body, 0)
+
+    def pass_on(self, s, first):
         n, p = self.n, self.pos
         low = 2 * p < n
         right = low if first else jnp.logical_not(low)
         c = jnp.where(right, n - 1 - s, s)
-        go = jnp.where(right, c > p, c < p)
-        has = jnp.where(right, p > 0, p < n - 1)
-        to = jnp.where(right, p + 1, p - 1)
-        slot = jnp.where(right, c, jnp.where(c == p - 1, n, c))
-        return c, go, has, to, slot
-
-    def copy(self, c, slot, to):
-        return remote(
-            self.chunk(c), self.slots.at[slot], self.send.at[c], self.recv.at[slot], self.device_of(to)
-        )
-
-    def arrive(self, slot):
-        self.copy(slot % self.n, slot, self.pos).wait_recv()
+        go = jnp.where(right, jnp.logical_and(c > p, p > 0), jnp.logical_and(c < p, p < n - 1))
+
+        @pl.when(go)
+        def _():
+            self.arrive(c)
+            mine = self.chunk(c)
+            mine[...] = mine[...] + self.slots[c]
+            self.launch(c, right)
 
     def step(self, s):
-        for first in (True, False):
-            c, go, has, to, slot = self.turn(s, first)
-
-            @pl.when(jnp.logical_and(go, has))
-            def _():
-                self.arrive(c)
-                mine = self.chunk(c)
-                mine[...] = mine[...] + self.slots[c]
-
-            @pl.when(go)
-            def _():
-                self.copy(c, slot, to).start()
+        if self.n > 2:
+            self.pass_on(s, True)
+            self.pass_on(s, False)
 
     def finish(self):
         n, p = self.n, self.pos
@@ -246,20 +257,22 @@
     ]
 
     def run(chain, lo, hi):
-        def body(s, _):
-            chain.step(s)
-            return 0
-
-        lax.fori_loop(lo, hi, body, 0)
+        if chain.n > 2:
+
+            def body(s, _):
+                chain.step(s)
+                return 0
+
+            lax.fori_loop(lo, hi, body, 0)
 
     for k in range(n_out):
         swaps[k].wait()
         mis[:, k * COLS : (k + 1) * COLS] = (d_out[k] + d_in[k]).astype(BF16)
         grad(k, st_b, mis[:, k * COLS : (k + 1) * COLS])
         if k == 0:
-            first_a.step(0)
-        elif k == 1:
-            run(bs[0], 0, nb - 1)
+            first_a.lead()
+        else:
+            bs[k - 1].lead()
 
     def back_block(i, _):
         at = pl.ds(pl.multiple_of(i * COLS, COLS), COLS)
@@ -290,6 +303,7 @@
         return 0
 
     lax.fori_loop(0, chip, send_rev, 0)
+    first_a.pass_on(0, True)
 
     def take_rev(k, carry):
         q = chips - 1 - k
@@ -328,18 +342,21 @@
 
     grad(n_out, ad_b, sig_b[...])
 
-    run(first_a, 1, na - 1)
+    bs[n_out - 1].lead()
+    first_a.pass_on(0, False)
     for k in range(n_out):
+        if k == 0:
+            run(first_a, 1, na - 1)
+        run(bs[k], 0, nb - 1)
         bs[k].finish()
-        if k + 1 < n_out:
-            run(bs[k + 1], 0, nb - 1)
+        as_[k].lead()
         if k == 0:
             first_a.finish()
-            run(then_b, 0, nb - 1)
-            run(as_[0], 0, na - 1)
+            then_b.lead()
         else:
-            run(as_[k], 0, na - 1)
             as_[k - 1].finish()
+        run(as_[k], 0, na - 1)
+    run(then_b, 0, nb - 1)
     then_b.finish()
     as_[n_out - 1].finish()
 

time: 167 us -> 152 us (0.910)
  Pallas kernels: 155 us -> 140 us
    pallas_call x1, Pallas kernels: 155 us -> 140 us  [per_device(): pl.pallas_call(functools.partial(kernel, na, nb, group, rows), out_shape=...]
where the time goes in v2:
time: 152 us
  Pallas kernels  140 us (92%)
  local copies, waits for them, and re-layouts  8.03 us (5%)
  other arithmetic  2.42 us (2%)
    pallas_call x1, Pallas kernels, per_device(): pl.pallas_call(functools.partial(kernel, na, nb, group, rows), out_shape=...  140 us
    concatenate x2, local copies, waits for them, and re-layouts, padded(): return jnp.concatenate([low, high], axis=1).reshape(lines, x.shape[2])  3.16 us

profile of v2, /device:TPU:0, one launch (start us, length us, event | category | flops | bytes accessed | tf_op | source)
XLA Modules:
  0.0 151.7 jit_solution(12504949365331897435)
XLA Ops:
  0.6 1.1 fusion
  1.8 0.1 pad_maximum_fusion
  1.9 0.0 copy-start.1
  1.9 2.1 %copy.21 = f32[64,8,768]{2,1,0:T(8,128)} copy(f32[64,8,768]{2,0,1:T(8,128)S(1)} %pad_maximum_fusion) | data formatting | bytes 3145728 | tf_op jit(solution)/shard_map/concatenate | solution.py:433
  4.0 0.0 copy-start.2
  4.0 0.0 copy-start.3
  4.0 0.0 copy-done.1
  4.1 1.1 copy.22
  5.2 0.0 copy-done.2
  5.2 0.0 copy-done.3
  5.2 0.2 cosine_multiply_fusion
  5.4 0.6 broadcast_in_dim.26.pole_ref
  6.0 0.6 broadcast_in_dim.27.gain_ref
  6.7 140.5 %shard_map.85 = (f32[256,768]{1,0:T(8,128)}, f32[256,256]{1,0:T(8,128)}, f32[8,2048]{1,0:T(8,128)}, f32[8,2048]{1,0:T(8,128)}) custom-call(f32[512,256]{1,0:T(8,128)} %bitcast.32, f32[512,768]{1,0:T(8,128)} %bitcast.30, f32[2,8,1024]{2,1,0:T(8,128)} %broadcast_in_dim.26.pole_ref, f32[8,2048]{1,0:T(8,128)} %broadcast_in_dim.27.gain_ref, ...), custom_call_target="tpu_custom_call" | custom-call | tf_op jit(solution)/shard_map/pallas_call | solution.py:488
  147.2 0.0 copy-start
  147.2 0.9 dynamic-slice_select_fusion.1
  148.1 0.1 copy.14
  148.2 0.7 reshape.133
  148.9 2.1 %copy.25 = f32[256,768]{1,0:T(8,128)} copy(f32[256,768]{1,0:T(8,128)} %get-tuple-element.25) | data formatting | bytes 1572864
  151.0 0.0 copy-done
  151.0 0.7 copy.26
  (8 shorter events, 0.1 us)
Async XLA Ops:
  1.9 2.1 %copy-start.1 = (bf16[4,64,256]{2,1,0:T(8,128)(2,1)S(1)}, bf16[4,64,256]{2,1,0:T(8,128)(2,1)}, u32[]{:S(2)}) copy-start(bf16[4,64,256]{2,1,0:T(8,128)(2,1)} %param.6) | copy-start | bytes 393220
  4.0 1.2 copy-start.2
  4.0 1.2 copy-start.3
  147.2 3.8 %copy-start = (f32[256,256]{1,0:T(8,128)S(1)}, f32[256,256]{1,0:T(8,128)}, u32[]{:S(2)}) copy-start(f32[256,256]{1,0:T(8,128)} %get-tuple-element.26) | copy-start | bytes 786436

commit v3 on v2

--- a/solution.py
+++ b/solution.py
@@ -101,11 +101,11 @@
 
 def kernel(
     na, nb, group, rows,
-    sig_ref, tgt_ref, pole_ref, gain_ref, in_hbm, out_hbm,
+    sig_ref, tgt_ref, pole_row, gain_ref, in_hbm, out_hbm,
     upd_ref, upi_ref, bnd_ref, bnr_ref,
     inm, outm, sig_in, sig_b, work, st_b, ad_b, d_out, d_in, mis,
     e_out, e_in, f_out, f_in, sq_out, sq_in,
-    gp, ys, zs, zz, zy,
+    gp, ys, zs, zz, zy, sig8, tgt8, pole_ref,
     ld_sem, pair_send, pair_recv, es, er, fs, fr, qs, qr,
     ysend, yrecv, zsend, zrecv, zzsend, zzrecv, zysend, zyrecv,
 ):
@@ -117,7 +117,7 @@
     pa = chip // nb
     pb = chip % nb
     mate = chip * 2 + 1 - core
-    half = pole_ref.shape[2]
+    half = pole_row.shape[2]
     width = 2 * half
     lines = 8 * group
     n_out = outm.shape[1] // COLS
@@ -133,6 +133,18 @@
     for load in loads:
         load.start()
 
+    def interleave(wide, x_ref):
+        wide[...] = jnp.zeros(wide.shape, F32)
+        for c in range(2):
+
+            @pl.when(core == c)
+            def _():
+                for m in range(4):
+                    wide[:, 4 * c + m, :] = x_ref[m].astype(F32)
+
+    interleave(sig8, sig_ref)
+    pole_ref[...] = jnp.broadcast_to(pole_row[...], pole_ref.shape)
+
     barrier = pltpu.get_barrier_semaphore()
 
     def greet(k, _):
@@ -143,12 +155,12 @@
     lax.fori_loop(1, n_tm, greet, 0)
     pl.semaphore_wait(barrier, n_tm - 1)
 
-    sig_copy = remote(sig_ref, sig_in, pair_send.at[0], pair_recv.at[0], mate)
+    sig_copy = remote(sig8, sig_in, pair_send.at[0], pair_recv.at[0], mate)
     sig_copy.start()
     for load in loads:
         load.wait()
     sig_copy.wait()
-    sig_b[...] = (sig_ref[...] + sig_in[...]).astype(BF16)
+    sig_b[...] = (sig8[...] + sig_in[...]).reshape(sig_b.shape).astype(BF16)
 
     def drive_block(i, _):
         at = pl.ds(pl.multiple_of(i * COLS, COLS), COLS)
@@ -186,6 +198,7 @@
         return 0
 
     lax.fori_loop(chip + 1, chips, send_fwd, 0)
+    interleave(tgt8, tgt_ref)
 
     def take_fwd(q, carry):
         r, m = carry
@@ -219,7 +232,7 @@
     for k in range(n_out):
         at = pl.ds(k * COLS, COLS)
         val = jnp.dot(st_b[...], outm[:, at], preferred_element_type=F32)
-        d_out[k] = val - tgt_ref[:, at]
+        d_out[k] = val - tgt8[:, :, at].reshape(lines, COLS)
         swap = remote(d_out.at[k], d_in.at[k], pair_send.at[1 + k], pair_recv.at[1 + k], mate)
         swap.start()
         swaps.append(swap)
@@ -426,21 +439,15 @@
     n_out = out_map.shape[1] // COLS
     lines = 2 * members * group
 
-    def padded(x):
-        x = jnp.transpose(x, (1, 0, 2)).astype(F32)
-        low = jnp.where(core == 0, x, 0.0)
-        high = jnp.where(core == 0, 0.0, x)
-        return jnp.concatenate([low, high], axis=1).reshape(lines, x.shape[2])
-
     def own(x):
         return lax.dynamic_index_in_dim(x.reshape(-1, 2, rows), core, 1, False).reshape(half)
 
     rate, angle = own(decay_rate), own(pole_angle)
     size = jnp.exp(-rate)
     pole = jnp.stack([size * jnp.cos(angle), size * jnp.sin(angle)])
-    pole = jnp.broadcast_to(pole[:, None, :], (2, 8, half))
+    pole = pole[:, None, :]
     gain = jnp.sqrt(-jnp.expm1(-2.0 * rate))
-    gain = jnp.broadcast_to(jnp.concatenate([gain, gain])[None], (8, width))
+    gain = jnp.concatenate([gain, gain])[None]
 
     vm = pl.BlockSpec(memory_space=pltpu.VMEM)
     anyw = pl.BlockSpec(memory_space=pl.ANY)
@@ -448,7 +455,7 @@
     scratch = [
         pltpu.VMEM((width, sensors), BF16),
         pltpu.VMEM((width, n_out * COLS), BF16),
-        pltpu.VMEM((lines, sensors), F32),
+        pltpu.VMEM((group, 8, sensors), F32),
         pltpu.VMEM((lines, sensors), BF16),
         pltpu.VMEM((group, 8, width), F32),
         pltpu.VMEM((lines, width), BF16),
@@ -467,6 +474,9 @@
         pltpu.VMEM((n_out, na + 1, rows, COLS), F32),
         pltpu.VMEM((na + 1, nb, rows, COLS), F32),
         pltpu.VMEM((nb + 1, rows, COLS), F32),
+        pltpu.VMEM((group, 8, sensors), F32),
+        pltpu.VMEM((group, 8, n_out * COLS), F32),
+        pltpu.VMEM((2, 8, half), F32),
         dma((2, chips)),
         dma((n_out + 2,)),
         dma((n_out + 2,)),
@@ -500,8 +510,8 @@
             collective_id=0, has_side_effects=True, vmem_limit_bytes=62 * 1024 * 1024
         ),
     )(
-        padded(signals),
-        padded(targets),
+        signals,
+        targets,
         pole,
         gain,
         in_map.reshape(chips, 2, rows, sensors),

time: 152 us -> 149 us (0.980)
    concatenate x2 -> x0, local copies, waits for them, and re-layouts: 3.16 us -> none  [padded(): return jnp.concatenate([low, high], axis=1).reshape(lines, x.shape[2])]
    unnamed x10 -> x2, local copies, waits for them, and re-layouts: 2.78 us -> 3.73 us
where the time goes in v3:
time: 149 us
  Pallas kernels  140 us (94%)
  local copies, waits for them, and re-layouts  6.54 us (4%)
  other arithmetic  1.67 us (1%)
    pallas_call x1, Pallas kernels, per_device(): pl.pallas_call(functools.partial(kernel, na, nb, group, rows), out_shape=...  140 us
    unnamed x2, local copies, waits for them, and re-layouts  3.73 us

profile of v3, /device:TPU:0, one launch (start us, length us, event | category | flops | bytes accessed | tf_op | source)
XLA Modules:
  0.0 148.6 jit_solution(3309420031399649555)
XLA Ops:
  0.6 0.7 reshape.119
  1.4 0.7 reshape.120
  2.1 0.2 cosine_multiply_fusion
  2.2 0.6 broadcast_in_dim.6.pole_row
  2.8 0.6 pad_maximum_fusion.2
  3.4 139.7 %shard_map.85 = (f32[256,768]{1,0:T(8,128)}, f32[256,256]{1,0:T(8,128)}, f32[8,2048]{1,0:T(8,128)}, f32[8,2048]{1,0:T(8,128)}) custom-call(bf16[4,64,256]{2,1,0:T(8,128)(2,1)} %sig_ref.1, bf16[4,64,768]{2,1,0:T(8,128)(2,1)} %tgt_ref.1, f32[2,1,1024]{2,1,0:T(1,128)} %broadcast_in_dim.6.pole_row, f32[1,2048]{1,0:T(1,128)} %bitcast.20, ...), custom_call_target="tpu_custom_call" | custom-call | tf_op jit(solution)/shard_map/pallas_call | solution.py:498
  143.2 0.9 dynamic-slice_select_fusion.1
  144.1 0.1 copy.10
  144.2 0.7 reshape.123
  144.9 2.1 %copy.17 = f32[256,768]{1,0:T(8,128)} copy(f32[256,768]{1,0:T(8,128)} %get-tuple-element.21) | data formatting | bytes 1572864
  147.0 1.7 %copy.18 = f32[256,256]{1,0:T(8,128)} copy(f32[256,256]{1,0:T(8,128)} %get-tuple-element.22) | data formatting | bytes 524288
  (3 shorter events, 0.0 us)

commit v4 on v3

--- a/solution.py
+++ b/solution.py
@@ -157,7 +157,7 @@
 
     sig_copy = remote(sig8, sig_in, pair_send.at[0], pair_recv.at[0], mate)
     sig_copy.start()
-    for load in loads:
+    for load in loads[0::2]:
         load.wait()
     sig_copy.wait()
     sig_b[...] = (sig8[...] + sig_in[...]).reshape(sig_b.shape).astype(BF16)
@@ -227,6 +227,9 @@
         return r, m
 
     lax.fori_loop(0, group // 2, state_step, (sr0, si0))
+
+    for load in loads[1::2]:
+        load.wait()
 
     swaps = []
     for k in range(n_out):

time: 149 us -> 149 us (level)
  no operation moved by 1% of the time
where the time goes in v4:
time: 149 us
  Pallas kernels  140 us (94%)
  local copies, waits for them, and re-layouts  6.54 us (4%)
  other arithmetic  1.67 us (1%)
    pallas_call x1, Pallas kernels, per_device(): pl.pallas_call(functools.partial(kernel, na, nb, group, rows), out_shape=...  140 us
    unnamed x2, local copies, waits for them, and re-layouts  3.73 us

profile of v4, /device:TPU:0, one launch (start us, length us, event | category | flops | bytes accessed | tf_op | source)
XLA Modules:
  0.0 148.6 jit_solution(3164865036316206972)
XLA Ops:
  0.6 0.7 reshape.119
  1.4 0.7 reshape.120
  2.1 0.2 cosine_multiply_fusion
  2.2 0.6 broadcast_in_dim.6.pole_row
  2.8 0.6 pad_maximum_fusion.2
  3.4 139.7 %shard_map.85 = (f32[256,768]{1,0:T(8,128)}, f32[256,256]{1,0:T(8,128)}, f32[8,2048]{1,0:T(8,128)}, f32[8,2048]{1,0:T(8,128)}) custom-call(bf16[4,64,256]{2,1,0:T(8,128)(2,1)} %sig_ref.1, bf16[4,64,768]{2,1,0:T(8,128)(2,1)} %tgt_ref.1, f32[2,1,1024]{2,1,0:T(1,128)} %broadcast_in_dim.6.pole_row, f32[1,2048]{1,0:T(1,128)} %bitcast.20, ...), custom_call_target="tpu_custom_call" | custom-call | tf_op jit(solution)/shard_map/pallas_call | solution.py:501
  143.2 0.9 dynamic-slice_select_fusion.1
  144.1 0.1 copy.10
  144.2 0.7 reshape.123
  144.9 2.1 %copy.17 = f32[256,768]{1,0:T(8,128)} copy(f32[256,768]{1,0:T(8,128)} %get-tuple-element.21) | data formatting | bytes 1572864
  147.0 1.7 %copy.18 = f32[256,256]{1,0:T(8,128)} copy(f32[256,256]{1,0:T(8,128)} %get-tuple-element.22) | data formatting | bytes 524288
  (3 shorter events, 0.0 us)
